TPU v7x, 32 devices: a whole 2x2x4 slice. The times are simulated.
32 devices in a mesh: rep: 2 (over x), tp: 16 (over z, y, core).
Axes of the slice: x: 2, y: 2, z: 4, core: 2. Of those that a mesh axis runs over, the one named last changes fastest.
Arguments:
- hidden_codes: bfloat16 [256, 34816], P('rep', 'tp'), parts along dimension 0, may hold values from -127 to 127, as said below
- hidden_scale: float32 [256], P('rep'), parts along dimension 0, may hold values from 0.0005 to 0.005
- down_codes: bfloat16 [34816, 16384], P('tp'), may hold values from -127 to 127, as said below
- weight_scale: float32 [16384], replicated, may hold values from 0.0006 to 0.006
- residual: bfloat16 [256, 16384], P('rep', 'tp'), parts along dimension 0, may hold values from -6 to 6
Outputs:
- mixed: bfloat16 [256, 16384], P('rep'), parts along dimension 0
There are 2 independent parts, one for each index of `rep`. A program takes and returns all parts, laid end to end along the dimension named above; an argument that names none is the same for every part. Nothing has to cross between parts.
Inputs may be any that keep to these rules, and one draw needn't show every extreme that they name: `hidden_codes`: whole numbers; every token's row holds a code of magnitude 127. `down_codes`: whole numbers; every output channel's column holds a code of magnitude 127.
All inputs are finite; a program needn't handle non-finite values. Where the computation divides by a largest or mean magnitude, that divisor is 1e-20 or more.
Results may differ from a plain program's by a relative error of at most 0.012.
Values may be sent and summed in bfloat16 or wider, within the bound.
A program may use at most 320 MiB of HBM per device.

v0:
```python
import jax
import jax.numpy as jnp
from jax import lax
from jax.sharding import PartitionSpec as P

BLOCK = 128


def shards(hidden_codes, hidden_scale, down_codes, weight_scale, residual):
    devices = lax.axis_size("tp")
    token_count = hidden_codes.shape[0]
    model_width = down_codes.shape[1]
    owned_cols = model_width // devices
    blocks = owned_cols // BLOCK
    weights = down_codes.reshape(down_codes.shape[0], devices, owned_cols)
    channel_scale = weight_scale.reshape(devices, 1, owned_cols)
    row_count = hidden_codes.shape[0]
    partial_value = jnp.einsum(
        "tf,fnc->ntc", hidden_codes, weights, preferred_element_type=jnp.float32
    )
    partial_value = partial_value * hidden_scale[None, :, None] * channel_scale
    grouped = partial_value.reshape(devices, row_count, blocks, BLOCK)
    block_scale = jnp.max(jnp.abs(grouped), axis=3) + 1e-06
    coded = (grouped / block_scale[..., None]).astype(jnp.bfloat16)
    coded, block_scale = (
        coded.reshape(devices, row_count, owned_cols),
        jnp.swapaxes(block_scale, 1, 2),
    )
    got_code, got_scale = (
        lax.all_to_all(coded, "tp", split_axis=0, concat_axis=0, tiled=True),
        lax.all_to_all(
            block_scale.astype(jnp.bfloat16), "tp", split_axis=0, concat_axis=0, tiled=True
        ).astype(block_scale.dtype),
    )
    received = got_code.reshape(devices, token_count, blocks, BLOCK).astype(jnp.float32)
    summed = jnp.einsum("ntbk,nbt->tbk", received, got_scale, precision=lax.Precision.HIGHEST)
    summed_rows = residual.astype(jnp.float32).reshape(token_count, blocks, BLOCK) + summed
    out_scale = jnp.max(jnp.abs(summed_rows), axis=2) + 1e-06
    out_code = (summed_rows / out_scale[..., None]).astype(jnp.bfloat16)
    codes_all, scales_all = (
        lax.all_gather(out_code.reshape(token_count, owned_cols), "tp", axis=1, tiled=True),
        lax.all_gather(out_scale.astype(jnp.bfloat16), "tp", axis=1, tiled=True).astype(
            out_scale.dtype
        ),
    )
    decoded_all = (
        codes_all.reshape(token_count, -1, BLOCK).astype(jnp.float32) * scales_all[..., None]
    )
    return decoded_all.reshape(token_count, model_width).astype(jnp.bfloat16)


def solution(mesh):
    placed = (P("rep", "tp"), P("rep"), P("tp", None), P(), P("rep", "tp"))
    return jax.shard_map(
        shards, mesh=mesh, in_specs=placed, out_specs=P("rep", None), check_vma=False
    )
```

profile of v0, /device:TPU:0, one launch (start us, length us, event | category | flops | bytes accessed | tf_op | source)
XLA Modules:
  0.0 307.3 jit_solution(8158808585980988955)
XLA Ops:
  6.5 0.0 copy-start
  6.5 0.9 mul.35
  7.5 0.0 copy-start.3
  7.5 84.4 %copy.20 = bf16[2176,16384]{0,1:T(8,128)(2,1)} copy(bf16[2176,16384]{1,0:T(8,128)(2,1)} %param.7) | data formatting | bytes 142606336 | tf_op jit(solution)/shard_map/reshape | solution.py:15
  91.8 0.0 copy-done
  91.8 0.0 copy-done.3
  91.8 30.3 %bitcast_reduce_fusion = (f32[16,128,8]{1,2,0:T(8,128)S(1)}, f32[16,1024,128]{2,1,0:T(8,128)}) fusion(f32[16,1024]{1,0:T(8,128)S(1)} %mul.35, f32[128]{0:T(128)S(1)} %copy-done.3, bf16[2176,16,1024]{0,2,1:T(8,128)(2,1)} %bitcast.2, bf16[128,2176]{1,0:T(8,128)(2,1)S(1)} %copy-done), kind=kOutput, calls=%fused_computation.4 | convolution fusion | flops 9135177728 | bytes 80380416 | tf_op jit(solution)/shard_map/tf,fnc->ntc/dot_general | solution.py:18
  122.1 0.6 convert_bitcast_fusion.1
  122.7 7.4 %all-to-all-start.1 = ((bf16[16,8,128]{2,1,0:T(8,128)(2,1)}), bf16[16,8,128]{2,1,0:T(8,128)(2,1)S(1)}, u32[]{:S(2)}, u32[]{:S(2)}) async-start(bf16[16,8,128]{2,1,0:T(8,128)(2,1)} %get-tuple-element.5), calls=%async_computation.1 | async-start | bytes 65536 | tf_op jit(solution)/shard_map/all_to_all | solution.py:31
  130.1 0.0 copy-start.2
  130.1 6.9 %fusion.1 = bf16[16,128,1024]{1,2,0:T(8,128)(2,1)} fusion(f32[16,1024,128]{2,1,0:T(8,128)} %get-tuple-element.8, f32[16,128,8]{1,2,0:T(8,128)S(1)} %get-tuple-element.6, f32[16,1024]{1,0:T(8,128)S(1)} %mul.35, f32[128]{0:T(128)S(1)} %copy-done.3), kind=kLoop, calls=%fused_computation.3 | loop fusion | flops 8388608 | bytes 12714496 | tf_op jit(solution)/shard_map/convert_element_type | solution.py:24
  137.0 0.0 all-to-all-done.1
  137.0 6.1 %all-to-all-start = ((bf16[16,128,1024]{1,2,0:T(8,128)(2,1)}), bf16[16,128,1024]{1,2,0:T(8,128)(2,1)}, u32[]{:S(2)}, u32[]{:S(2)}) async-start(bf16[16,128,1024]{1,2,0:T(8,128)(2,1)} %fusion.1), calls=%async_computation | async-start | bytes 8388608 | tf_op jit(solution)/shard_map/all_to_all | solution.py:30
  143.1 0.0 all-gather.2.cloned.1.call-start
  143.1 0.0 copy-done.2
  143.2 0.1 copy.23
  143.3 77.4 %all-to-all-done = bf16[16,128,1024]{1,2,0:T(8,128)(2,1)} async-done(((bf16[16,128,1024]{1,2,0:T(8,128)(2,1)}), bf16[16,128,1024]{1,2,0:T(8,128)(2,1)}, u32[]{:S(2)}, u32[]{:S(2)}) %all-to-all-start) | async-done | bytes 4194336 | tf_op jit(solution)/shard_map/all_to_all | solution.py:30
  220.8 3.3 %multiply_reduce_fusion = f32[128,8,128]{0,2,1:T(8,128)S(1)} fusion(bf16[128,8,16,128]{0,3,1,2:T(8,128)(2,1)} %bitcast, f32[128,8,16]{0,1,2:T(8,128)S(1)} %bitcast_convert_fusion), kind=kLoop, calls=%fused_computation.6 | loop fusion | flops 6160384 | bytes 4784128
  224.1 0.2 copy.19
  224.3 0.1 bitcast_add_fusion
  224.4 0.2 abs_reduce_fusion
  224.6 0.2 divide_convert_fusion
  224.8 0.8 copy.28
  225.6 0.0 all-gather.2.cloned.1.call-update
  225.6 0.1 copy.11
  225.6 35.8 %all_gather.7 = bf16[128,128]{0,1:T(8,128)(2,1)S(1)} all-gather(bf16[128,8]{0,1:T(8,128)(2,1)S(1)} %copy.11), channel_id=1, replica_groups=mesh['rep'=2,'tp'=16] {'tp'}, dimensions={1}, use_global_device_ids=true | all-gather | bytes 34816 | tf_op jit(solution)/shard_map/all_gather | solution.py:42
  261.5 0.1 copy.12
  261.6 29.7 %all-gather.2.cloned.1.call-done = bf16[128,16384]{1,0:T(8,128)(2,1)} async-done(((bf16[128,1024]{1,0:T(8,128)(2,1)}), bf16[128,16384]{1,0:T(8,128)(2,1)}) %all-gather.2.cloned.1.call-update) | async-done | bytes 4194320 | tf_op jit(solution)/shard_map/all_gather | solution.py:41
  291.3 0.0 copy-start.1
  291.3 2.3 mul.39
  293.6 0.0 copy-done.1
  293.6 6.9 %fusion = bf16[128,16384]{1,0:T(8,128)(2,1)} fusion(f32[16,8,128,128]{3,2,1,0:T(8,128)S(1)} %bitcast.38, bf16[128,16384]{1,0:T(8,128)(2,1)S(1)} %copy-done.1), kind=kLoop, calls=%fused_computation.1 | loop fusion | flops 6291456 | bytes 16777216 | tf_op jit(solution)/shard_map/convert_element_type | solution.py:49
  (3 shorter events, 0.1 us)
Async XLA Ops:
  6.5 85.3 %copy-start = (bf16[128,2176]{1,0:T(8,128)(2,1)S(1)}, bf16[128,2176]{1,0:T(8,128)(2,1)}, u32[]{:S(2)}) copy-start(bf16[128,2176]{1,0:T(8,128)(2,1)} %param.5) | copy-start | bytes 1671172
  7.5 84.4 %copy-start.3 = (f32[128]{0:T(128)S(1)}, f32[128]{0:T(128)}, u32[]{:S(2)}) copy-start(f32[128]{0:T(128)} %param.6) | copy-start | bytes 1540
  122.7 14.3 %all-to-all-start.1 = ((bf16[16,8,128]{2,1,0:T(8,128)(2,1)}), bf16[16,8,128]{2,1,0:T(8,128)(2,1)S(1)}, u32[]{:S(2)}, u32[]{:S(2)}) async-start(bf16[16,8,128]{2,1,0:T(8,128)(2,1)} %get-tuple-element.5), calls=%async_computation.1 | async-start | bytes 65536 | tf_op jit(solution)/shard_map/all_to_all | solution.py:31
  130.1 13.0 %copy-start.2 = (bf16[128,1024]{1,0:T(8,128)(2,1)S(1)}, bf16[128,1024]{1,0:T(8,128)(2,1)}, u32[]{:S(2)}) copy-start(bf16[128,1024]{1,0:T(8,128)(2,1)} %param.9) | copy-start | bytes 786436
  137.0 83.7 %all-to-all-start = ((bf16[16,128,1024]{1,2,0:T(8,128)(2,1)}), bf16[16,128,1024]{1,2,0:T(8,128)(2,1)}, u32[]{:S(2)}, u32[]{:S(2)}) async-start(bf16[16,128,1024]{1,2,0:T(8,128)(2,1)} %fusion.1), calls=%async_computation | async-start | bytes 8388608 | tf_op jit(solution)/shard_map/all_to_all | solution.py:30
  143.1 148.2 %all-gather.2.cloned.1.call-start = ((), (), s32[]{:S(2)}) async-start(), calls=%async_computation.2 | async-start | bytes 4456448 | tf_op jit(solution)/shard_map/all_gather | solution.py:41
  291.3 2.3 copy-start.1
Sparse Core Ops, SparseCore 0:
  225.7 65.5 all-gather.1
where the time goes:
time: 310 us; the launch traced here: 307 us
  waiting for transfers between devices  107 us (35%)
  local copies, waits for them, and re-layouts  88.8 us (29%)
  blocking collectives  35.8 us (12%)
  matrix products  30.3 us (10%)
  other arithmetic  18.2 us (6%)
  starting transfers between devices  13.5 us (4%)
  between operations  13.5 us (4%)
    reshape x1, local copies, waits for them, and re-layouts, shards(): weights = down_codes.reshape(down_codes.shape[0], devices, owned_cols)  84.4 us
    all_to_all x1, waiting for transfers between devices, shards(): lax.all_to_all(coded, 'tp', split_axis=0, concat_axis=0, tiled=True)  77.4 us
    all_gather x1, blocking collectives, shards(): lax.all_gather(out_scale.astype(jnp.bfloat16), 'tp', axis=1, tiled=True)  35.8 us
    dot_general x1, matrix products, shards(): jnp.einsum('tf,fnc->ntc', hidden_codes, weights, preferred_element_type=j...  30.3 us
    all_gather x1, waiting for transfers between devices, shards(): lax.all_gather(out_code.reshape(token_count, owned_cols), 'tp', axis=1, t...  29.7 us
    all_to_all x1, starting transfers between devices, shards(): lax.all_to_all(block_scale.astype(jnp.bfloat16), 'tp', split_axis=0, conc...  7.38 us
    convert_element_type x1, other arithmetic, shards(): coded = (grouped / block_scale[..., None]).astype(jnp.bfloat16)  6.87 us
    convert_element_type x1, other arithmetic, shards(): return decoded_all.reshape(token_count, model_width).astype(jnp.bfloat16)  6.87 us
  transfers between devices with their start and end apart: 3, of which 2 were waited for; matrix products, arithmetic and copies ran while one was open for 2% of the time, Pallas kernels for 0%

commit v1 on v0

v1 whole, which is shorter than its diff:
```python
import functools

import jax
import jax.numpy as jnp
from jax import lax
from jax.experimental import pallas as pl
from jax.experimental.pallas import tpu as pltpu
from jax.sharding import PartitionSpec as P

BLOCK = 128
CORES = 2
WIDTH = 256
BUFFERS = 8
MESH = pl.DeviceIdType.MESH


def grid_of(devices):
    chips = devices // CORES
    inner = 1
    while (2 * inner) ** 2 <= chips:
        inner *= 2
    return chips // inner, inner


def kernel(
    nz, ny, width, chunks,
    hid_ref, hs_ref, ws_ref, res_ref, w_ref, out_ref,
    wbuf, mine, cs, cr, ys, yr, zs, zr, fin,
    wsem, cs_sem, cr_sem, ys_sem, yr_sem, zs_sem, zr_sem, loc_sem,
    gzs_sem, gzr_sem, gys_sem, gyr_sem, gcs_sem, gcr_sem,
):
    me = lax.axis_index("tp")
    c = lax.rem(me, CORES)
    y = lax.rem(me // CORES, ny)
    z = me // (CORES * ny)
    owned = chunks * width
    tiles = ny * nz
    total_tiles = chunks * 2 * tiles

    def device(zi, yi, ci):
        return {"tp": (zi * ny + yi) * CORES + ci}

    partner = device(z, y, 1 - c)
    y_of = [lax.rem(y + j, ny) for j in range(ny)]
    z_of = [lax.rem(z + j, nz) for j in range(nz)]

    def column(t):
        k = t // (2 * tiles)
        h = lax.rem(t // tiles, 2)
        i = lax.rem(t, tiles)
        core = jnp.where(h == 0, 1 - c, c)
        owner = (lax.rem(i, nz) * ny + i // nz) * CORES + core
        return pl.multiple_of(owner * owned + k * width, 128)

    def fetch(t):
        slot = lax.rem(t, BUFFERS)
        return pltpu.make_async_copy(
            w_ref.at[:, pl.ds(column(t), width)], wbuf.at[slot], wsem.at[slot]
        )

    for t in range(min(BUFFERS - 1, total_tiles)):
        fetch(jnp.int32(t)).start()

    barrier = pltpu.get_barrier_semaphore()
    peers = [partner]
    peers += [device(z, y_of[j], c) for j in range(1, ny)]
    peers += [device(z_of[j], y, c) for j in range(1, nz)]
    for peer in peers:
        pl.semaphore_signal(barrier, inc=1, device_id=peer, device_id_type=MESH)
    pl.semaphore_wait(barrier, len(peers))

    def remote(src, dst, send, recv, peer):
        return pltpu.make_async_remote_copy(
            src_ref=src, dst_ref=dst, send_sem=send, recv_sem=recv,
            device_id=peer, device_id_type=MESH,
        )

    def core_copy(k):
        return remote(cs.at[k], cr.at[k], cs_sem.at[k], cr_sem.at[k], partner)

    def y_copy(k, j):
        return remote(ys.at[k, j - 1], yr.at[k, j - 1], ys_sem.at[k, j - 1],
                      yr_sem.at[k, j - 1], device(z, y_of[j], c))

    def z_copy(k, j):
        return remote(zs.at[k, j - 1], zr.at[k, j - 1], zs_sem.at[k, j - 1],
                      zr_sem.at[k, j - 1], device(z_of[j], y, c))

    def local_copy(k):
        return pltpu.make_async_copy(fin.at[k], out_ref.at[k, c, y, z], loc_sem.at[k])

    def gather_z(k, j):
        block = out_ref.at[k, c, y, z]
        return remote(fin.at[k], block, gzs_sem.at[k, j - 1], gzr_sem.at[k, j - 1],
                      device(z_of[j], y, c))

    def gather_y(k, j):
        block = out_ref.at[k, c, y]
        return remote(block, block, gys_sem.at[k, j - 1], gyr_sem.at[k, j - 1],
                      device(z, y_of[j], c))

    def gather_core(k):
        block = out_ref.at[k, c]
        return remote(block, block, gcs_sem.at[k], gcr_sem.at[k], partner)

    def multiply(k, h):
        first = (k * 2 + h) * tiles

        @pl.loop(0, tiles)
        def _(i):
            t = first + i

            @pl.when(t + BUFFERS - 1 < total_tiles)
            def _():
                fetch(t + BUFFERS - 1).start()

            fetch(t).wait()
            value = jnp.dot(
                hid_ref[...], wbuf[lax.rem(t, BUFFERS)], preferred_element_type=jnp.float32
            )
            value = value * hs_ref[...] * ws_ref[:, pl.ds(column(t), width)]
            if h == 0:
                cs[k, i // nz, lax.rem(i, nz)] = value.astype(cs.dtype)
            else:
                mine[k, i // nz, lax.rem(i, nz)] = value

    def send_y(k):
        core_copy(k).wait_recv()
        for j in range(1, ny):
            @pl.loop(0, nz)
            def _(b):
                ys[k, j - 1, b] = (
                    mine[k, y_of[j], b] + cr[k, y_of[j], b].astype(jnp.float32)
                ).astype(ys.dtype)

            y_copy(k, j).start()

        @pl.loop(0, nz)
        def _(b):
            mine[k, y, b] += cr[k, y, b].astype(jnp.float32)

    def send_z(k):
        for j in range(1, ny):
            y_copy(k, j).wait_recv()

        def total(b):
            value = mine[k, y, b]
            for j in range(1, ny):
                value += yr[k, j - 1, b].astype(jnp.float32)
            return value

        for j in range(1, nz):
            zs[k, j - 1] = total(z_of[j]).astype(zs.dtype)
            z_copy(k, j).start()
        mine[k, y, z] = total(z)

    def finish(k):
        value = mine[k, y, z] + res_ref[:, k * width:(k + 1) * width].astype(jnp.float32)
        for j in range(1, nz):
            z_copy(k, j).wait_recv()
            value += zr[k, j - 1].astype(jnp.float32)
        for b in range(width // BLOCK):
            part = value[:, b * BLOCK:(b + 1) * BLOCK]
            scale = jnp.max(jnp.abs(part), axis=1, keepdims=True) + 1e-6
            code = (part / scale).astype(jnp.bfloat16)
            fin[k, :, b * BLOCK:(b + 1) * BLOCK] = (
                code.astype(jnp.float32) * scale
            ).astype(fin.dtype)
        for j in range(1, nz):
            gather_z(k, j).start()
        local_copy(k).start()

    def pass_y(k):
        local_copy(k).wait()
        for j in range(1, nz):
            gather_z(k, j).wait_recv()
        for j in range(1, ny):
            gather_y(k, j).start()

    def pass_core(k):
        for j in range(1, ny):
            gather_y(k, j).wait_recv()
        gather_core(k).start()

    def drain(k):
        gather_core(k).wait()
        core_copy(k).wait_send()
        for j in range(1, ny):
            y_copy(k, j).wait_send()
            gather_y(k, j).wait_send()
        for j in range(1, nz):
            z_copy(k, j).wait_send()
            gather_z(k, j).wait_send()

    stages = ((send_y, 1), (send_z, 3), (finish, 5), (pass_y, 7), (pass_core, 9))
    for u in range(2 * chunks + 8):
        k, h = u // 2, u % 2
        if k < chunks:
            multiply(k, h)
            if h == 0:
                core_copy(k).start()
        for stage, lag in reversed(stages):
            if (u - lag) % 2 == 0 and 0 <= (u - lag) // 2 < chunks:
                stage((u - lag) // 2)
    for k in range(chunks):
        drain(k)


def shards(hidden_codes, hidden_scale, down_codes, weight_scale, residual):
    devices = lax.axis_size("tp")
    nz, ny = grid_of(devices)
    rows, depth = hidden_codes.shape
    model_width = down_codes.shape[1]
    owned = model_width // devices
    width = min(WIDTH, owned)
    chunks = owned // width
    bf16, f32 = jnp.bfloat16, jnp.float32
    vmem = pl.BlockSpec(memory_space=pltpu.VMEM)
    dma = pltpu.SemaphoreType.DMA
    tile = (rows, width)
    got = pl.pallas_call(
        functools.partial(kernel, nz, ny, width, chunks),
        out_shape=jax.ShapeDtypeStruct((chunks, CORES, ny, nz) + tile, bf16),
        in_specs=[vmem, vmem, vmem, vmem, pl.BlockSpec(memory_space=pl.ANY)],
        out_specs=pl.BlockSpec(memory_space=pl.ANY),
        scratch_shapes=[
            pltpu.VMEM((BUFFERS, depth, width), bf16),
            pltpu.VMEM((chunks, ny, nz) + tile, f32),
            pltpu.VMEM((chunks, ny, nz) + tile, bf16),
            pltpu.VMEM((chunks, ny, nz) + tile, bf16),
            pltpu.VMEM((chunks, ny - 1, nz) + tile, bf16),
            pltpu.VMEM((chunks, ny - 1, nz) + tile, bf16),
            pltpu.VMEM((chunks, nz - 1) + tile, bf16),
            pltpu.VMEM((chunks, nz - 1) + tile, bf16),
            pltpu.VMEM((chunks,) + tile, bf16),
            dma((BUFFERS,)), dma((chunks,)), dma((chunks,)),
            dma((chunks, ny - 1)), dma((chunks, ny - 1)),
            dma((chunks, nz - 1)), dma((chunks, nz - 1)), dma((chunks,)),
            dma((chunks, nz - 1)), dma((chunks, nz - 1)),
            dma((chunks, ny - 1)), dma((chunks, ny - 1)),
            dma((chunks,)), dma((chunks,)),
        ],
        compiler_params=pltpu.CompilerParams(
            collective_id=0, has_side_effects=True, vmem_limit_bytes=48 * 1024 * 1024
        ),
        cost_estimate=pl.CostEstimate(
            flops=2 * rows * depth * model_width,
            bytes_accessed=2 * depth * model_width,
            transcendentals=0,
        ),
    )(hidden_codes, hidden_scale[:, None], weight_scale[None, :], residual, down_codes)
    got = jnp.transpose(got, (4, 3, 2, 1, 0, 5))
    return got.reshape(rows, model_width)


def solution(mesh):
    placed = (P("rep", "tp"), P("rep"), P("tp", None), P(), P("rep", "tp"))
    return jax.shard_map(
        shards, mesh=mesh, in_specs=placed, out_specs=P("rep", None), check_vma=False
    )
```

time: 310 us -> 94.2 us (0.30)
  waiting for transfers between devices: 107 us -> 0 us
  Pallas kernels: 0 us -> 74.5 us
  local copies, waits for them, and re-layouts: 88.8 us -> 19.2 us
  blocking collectives: 35.8 us -> 0 us
  matrix products: 30.3 us -> 0 us
  other arithmetic: 18.2 us -> 0 us
  starting transfers between devices: 13.5 us -> 0 us
  between operations: 13.5 us -> 0.03 us
    reshape x1, local copies, waits for them, and re-layouts: 84.4 us -> 6.36 us  [shards(): return got.reshape(rows, model_width)]
    all_to_all x2 -> x0, waiting for transfers between devices: 77.4 us -> none  [the longest x1 77.4 us: shards(): lax.all_to_all(coded, 'tp', split_axis=0, concat_axis=0, tiled=True)]
    pallas_call x0 -> x1, Pallas kernels: none -> 74.5 us  [shards(): pl.pallas_call(functools.partial(kernel, nz, ny, width, chunks), out_shap...]
    all_gather x1 -> x0, blocking collectives: 35.8 us -> none  [shards(): lax.all_gather(out_scale.astype(jnp.bfloat16), 'tp', axis=1, tiled=True)]
    dot_general x1 -> x0, matrix products: 30.3 us -> none  [shards(): jnp.einsum('tf,fnc->ntc', hidden_codes, weights, preferred_element_type=j...]
    all_gather x1 -> x0, waiting for transfers between devices: 29.7 us -> none  [shards(): lax.all_gather(out_code.reshape(token_count, owned_cols), 'tp', axis=1, t...]
    convert_element_type x4 -> x0, other arithmetic: 14.6 us -> none  [the longest x1 6.87 us: shards(): coded = (grouped / block_scale[..., None]).astype(jnp.bfloat16)]
    all_to_all x2 -> x0, starting transfers between devices: 13.4 us -> none  [the longest x1 7.38 us: shards(): lax.all_to_all(block_scale.astype(jnp.bfloat16), 'tp', split_axis=0, conc...]
  transfers between devices with their start and end apart: 3 -> 0, of which waited for: 2 -> 0; matrix products, arithmetic and copies ran while one was open for 2% -> 0% of each run, Pallas kernels for 0% -> 0%
where the time goes in v1:
time: 94.2 us; the launch traced here: 93.7 us
  Pallas kernels  74.5 us (79%)
  local copies, waits for them, and re-layouts  19.2 us (20%)
    pallas_call x1, Pallas kernels, shards(): pl.pallas_call(functools.partial(kernel, nz, ny, width, chunks), out_shap...  74.5 us
    transpose x1, local copies, waits for them, and re-layouts, shards(): got = jnp.transpose(got, (4, 3, 2, 1, 0, 5))  7.25 us
    reshape x1, local copies, waits for them, and re-layouts, shards(): return got.reshape(rows, model_width)  6.36 us
    unnamed x8, local copies, waits for them, and re-layouts  4.84 us

profile of v1, /device:TPU:0, one launch (start us, length us, event | category | flops | bytes accessed | tf_op | source)
XLA Modules:
  0.0 93.7 jit_solution(2150010231334672690)
XLA Ops:
  0.0 0.8 copy.7.hs_ref
  0.8 0.0 copy-start.1
  0.8 1.0 %copy-done.1 = bf16[128,2176]{1,0:T(8,128)(2,1)S(1)} copy-done((bf16[128,2176]{1,0:T(8,128)(2,1)S(1)}, bf16[128,2176]{1,0:T(8,128)(2,1)}, u32[]{:S(2)}) %copy-start.1) | copy-done | bytes 557080
  1.8 0.0 copy-start.2
  1.8 0.9 %copy-done.2 = bf16[128,1024]{1,0:T(8,128)(2,1)S(1)} copy-done((bf16[128,1024]{1,0:T(8,128)(2,1)S(1)}, bf16[128,1024]{1,0:T(8,128)(2,1)}, u32[]{:S(2)}) %copy-start.2) | copy-done | bytes 262168
  2.8 0.0 copy-start.3
  2.8 0.8 copy-done.3
  3.6 74.5 %shard_map.55 = bf16[4,2,2,4,128,256]{5,4,3,2,1,0:T(8,128)(2,1)S(1)} custom-call(bf16[128,2176]{1,0:T(8,128)(2,1)S(1)} %copy-done.1, f32[128,1]{1,0:T(8,128)S(1)} %copy.7.hs_ref, f32[1,16384]{1,0:T(1,128)S(1)} %bitcast.5, bf16[128,1024]{1,0:T(8,128)(2,1)S(1)} %copy-done.2, bf16[2176,16384]{1,0:T(8,128)(2,1)} %w_ref.1), custom_call_target="tpu_custom_call" | custom-call | flops 9126805504 | bytes 71303168 | tf_op jit(solution)/shard_map/pallas_call | solution.py:221
  78.1 0.0 copy-start
  78.1 2.0 %copy-done = bf16[4,2,2,4,128,256]{5,4,3,2,1,0:T(8,128)(2,1)} copy-done((bf16[4,2,2,4,128,256]{5,4,3,2,1,0:T(8,128)(2,1)}, bf16[4,2,2,4,128,256]{5,4,3,2,1,0:T(8,128)(2,1)S(1)}, u32[]{:S(2)}) %copy-start) | copy-done | bytes 4194328
  80.1 7.2 %copy.8 = bf16[128,4,2,2,4,256]{0,5,4,3,2,1:T(8,128)(2,1)} copy(bf16[128,4,2,2,4,256]{5,0,1,2,3,4:T(8,128)(2,1)} %bitcast.4) | data formatting | bytes 8388608 | tf_op jit(solution)/shard_map/transpose | solution.py:252
  87.3 6.4 %copy.9 = bf16[128,16384]{1,0:T(8,128)(2,1)} copy(bf16[128,16384]{0,1:T(8,128)(2,1)} %bitcast.6) | data formatting | bytes 8388608 | tf_op jit(solution)/shard_map/reshape | solution.py:253
Async XLA Ops:
  0.8 1.1 %copy-start.1 = (bf16[128,2176]{1,0:T(8,128)(2,1)S(1)}, bf16[128,2176]{1,0:T(8,128)(2,1)}, u32[]{:S(2)}) copy-start(bf16[128,2176]{1,0:T(8,128)(2,1)} %hid_ref.1) | copy-start | bytes 1671172
  1.8 0.9 %copy-start.2 = (bf16[128,1024]{1,0:T(8,128)(2,1)S(1)}, bf16[128,1024]{1,0:T(8,128)(2,1)}, u32[]{:S(2)}) copy-start(bf16[128,1024]{1,0:T(8,128)(2,1)} %res_ref.1) | copy-start | bytes 786436
  2.8 0.8 copy-start.3
  78.1 2.0 %copy-start = (bf16[4,2,2,4,128,256]{5,4,3,2,1,0:T(8,128)(2,1)}, bf16[4,2,2,4,128,256]{5,4,3,2,1,0:T(8,128)(2,1)S(1)}, u32[]{:S(2)}) copy-start(bf16[4,2,2,4,128,256]{5,4,3,2,1,0:T(8,128)(2,1)S(1)} %shard_map.55) | copy-start | bytes 12582916

commit v2 on v1

--- a/solution.py
+++ b/solution.py
@@ -43,6 +43,8 @@
     partner = device(z, y, 1 - c)
     y_of = [lax.rem(y + j, ny) for j in range(ny)]
     z_of = [lax.rem(z + j, nz) for j in range(nz)]
+    y_back = [lax.rem(y + ny - j, ny) for j in range(ny)]
+    z_back = [lax.rem(z + nz - j, nz) for j in range(nz)]
 
     def column(t):
         k = t // (2 * tiles)
@@ -86,22 +88,25 @@
         return remote(zs.at[k, j - 1], zr.at[k, j - 1], zs_sem.at[k, j - 1],
                       zr_sem.at[k, j - 1], device(z_of[j], y, c))
 
+    def block_of(k, yi, zi):
+        owner = (zi * ny + yi) * CORES + c
+        return out_ref.at[:, pl.ds(pl.multiple_of(owner * owned + k * width, 128), width)]
+
     def local_copy(k):
-        return pltpu.make_async_copy(fin.at[k], out_ref.at[k, c, y, z], loc_sem.at[k])
+        return pltpu.make_async_copy(fin.at[k], block_of(k, y, z), loc_sem.at[k])
 
     def gather_z(k, j):
-        block = out_ref.at[k, c, y, z]
-        return remote(fin.at[k], block, gzs_sem.at[k, j - 1], gzr_sem.at[k, j - 1],
-                      device(z_of[j], y, c))
-
-    def gather_y(k, j):
-        block = out_ref.at[k, c, y]
-        return remote(block, block, gys_sem.at[k, j - 1], gyr_sem.at[k, j - 1],
+        return remote(fin.at[k], block_of(k, y, z), gzs_sem.at[k, j - 1],
+                      gzr_sem.at[k, j - 1], device(z_of[j], y, c))
+
+    def gather_y(k, j, b):
+        block = block_of(k, y, z_back[b])
+        return remote(block, block, gys_sem.at[k, j - 1, b], gyr_sem.at[k, j - 1, b],
                       device(z, y_of[j], c))
 
-    def gather_core(k):
-        block = out_ref.at[k, c]
-        return remote(block, block, gcs_sem.at[k], gcr_sem.at[k], partner)
+    def gather_core(k, a, b):
+        block = block_of(k, y_back[a], z_back[b])
+        return remote(block, block, gcs_sem.at[k, a, b], gcr_sem.at[k, a, b], partner)
 
     def multiply(k, h):
         first = (k * 2 + h) * tiles
@@ -171,23 +176,30 @@
         local_copy(k).start()
 
     def pass_y(k):
-        local_copy(k).wait()
-        for j in range(1, nz):
-            gather_z(k, j).wait_recv()
-        for j in range(1, ny):
-            gather_y(k, j).start()
+        for b in range(nz):
+            if b == 0:
+                local_copy(k).wait()
+            else:
+                gather_z(k, b).wait_recv()
+            for j in range(1, ny):
+                gather_y(k, j, b).start()
+            gather_core(k, 0, b).start()
 
     def pass_core(k):
-        for j in range(1, ny):
-            gather_y(k, j).wait_recv()
-        gather_core(k).start()
+        for b in range(nz):
+            for j in range(1, ny):
+                gather_y(k, j, b).wait_recv()
+                gather_core(k, j, b).start()
 
     def drain(k):
-        gather_core(k).wait()
+        for a in range(ny):
+            for b in range(nz):
+                gather_core(k, a, b).wait()
         core_copy(k).wait_send()
         for j in range(1, ny):
             y_copy(k, j).wait_send()
-            gather_y(k, j).wait_send()
+            for b in range(nz):
+                gather_y(k, j, b).wait_send()
         for j in range(1, nz):
             z_copy(k, j).wait_send()
             gather_z(k, j).wait_send()
@@ -220,7 +232,7 @@
     tile = (rows, width)
     got = pl.pallas_call(
         functools.partial(kernel, nz, ny, width, chunks),
-        out_shape=jax.ShapeDtypeStruct((chunks, CORES, ny, nz) + tile, bf16),
+        out_shape=jax.ShapeDtypeStruct((rows, model_width), bf16),
         in_specs=[vmem, vmem, vmem, vmem, pl.BlockSpec(memory_space=pl.ANY)],
         out_specs=pl.BlockSpec(memory_space=pl.ANY),
         scratch_shapes=[
@@ -237,8 +249,8 @@
             dma((chunks, ny - 1)), dma((chunks, ny - 1)),
             dma((chunks, nz - 1)), dma((chunks, nz - 1)), dma((chunks,)),
             dma((chunks, nz - 1)), dma((chunks, nz - 1)),
-            dma((chunks, ny - 1)), dma((chunks, ny - 1)),
-            dma((chunks,)), dma((chunks,)),
+            dma((chunks, ny - 1, nz)), dma((chunks, ny - 1, nz)),
+            dma((chunks, ny, nz)), dma((chunks, ny, nz)),
         ],
         compiler_params=pltpu.CompilerParams(
             collective_id=0, has_side_effects=True, vmem_limit_bytes=48 * 1024 * 1024
@@ -249,8 +261,7 @@
             transcendentals=0,
         ),
     )(hidden_codes, hidden_scale[:, None], weight_scale[None, :], residual, down_codes)
-    got = jnp.transpose(got, (4, 3, 2, 1, 0, 5))
-    return got.reshape(rows, model_width)
+    return got
 
 
 def solution(mesh):

time: 94.2 us -> 80.1 us (0.85)
  local copies, waits for them, and re-layouts: 19.2 us -> 5.61 us
    transpose x1 -> x0, local copies, waits for them, and re-layouts: 7.25 us -> none  [shards(): got = jnp.transpose(got, (4, 3, 2, 1, 0, 5))]
    reshape x1 -> x0, local copies, waits for them, and re-layouts: 6.36 us -> none  [shards(): return got.reshape(rows, model_width)]
    unnamed x8 -> x7, local copies, waits for them, and re-layouts: 4.84 us -> 4.85 us
where the time goes in v2:
time: 80.1 us; the launch traced here: 79.9 us
  Pallas kernels  74.2 us (93%)
  local copies, waits for them, and re-layouts  5.61 us (7%)
    pallas_call x1, Pallas kernels, shards(): pl.pallas_call(functools.partial(kernel, nz, ny, width, chunks), out_shap...  74.2 us
    unnamed x7, local copies, waits for them, and re-layouts  4.85 us

profile of v2, /device:TPU:0, one launch (start us, length us, event | category | flops | bytes accessed | tf_op | source)
XLA Modules:
  0.0 79.9 jit_solution(3769182360960644604)
XLA Ops:
  0.0 0.8 copy.6.hs_ref
  0.8 0.0 copy-start
  0.8 1.0 %copy-done = bf16[128,2176]{1,0:T(8,128)(2,1)S(1)} copy-done((bf16[128,2176]{1,0:T(8,128)(2,1)S(1)}, bf16[128,2176]{1,0:T(8,128)(2,1)}, u32[]{:S(2)}) %copy-start) | copy-done | bytes 557080
  1.8 0.0 copy-start.1
  1.8 0.9 %copy-done.1 = bf16[128,1024]{1,0:T(8,128)(2,1)S(1)} copy-done((bf16[128,1024]{1,0:T(8,128)(2,1)S(1)}, bf16[128,1024]{1,0:T(8,128)(2,1)}, u32[]{:S(2)}) %copy-start.1) | copy-done | bytes 262168
  2.8 0.0 copy-start.2
  2.8 0.8 %copy-done.2 = f32[16384]{0:T(1024)S(1)} copy-done((f32[16384]{0:T(1024)S(1)}, f32[16384]{0:T(1024)}, u32[]{:S(2)}) %copy-start.2) | copy-done | bytes 65560
  3.6 74.2 %shard_map.55 = bf16[128,16384]{1,0:T(8,128)(2,1)S(1)} custom-call(bf16[128,2176]{1,0:T(8,128)(2,1)S(1)} %copy-done, f32[128,1]{1,0:T(8,128)S(1)} %copy.6.hs_ref, f32[1,16384]{1,0:T(1,128)S(1)} %bitcast.2, bf16[128,1024]{1,0:T(8,128)(2,1)S(1)} %copy-done.1, bf16[2176,16384]{1,0:T(8,128)(2,1)} %w_ref.1), custom_call_target="tpu_custom_call" | custom-call | flops 9126805504 | bytes 71303168 | tf_op jit(solution)/shard_map/pallas_call | solution.py:233
  77.8 2.0 %copy.8 = bf16[128,16384]{1,0:T(8,128)(2,1)} copy(bf16[128,16384]{1,0:T(8,128)(2,1)S(1)} %shard_map.55) | data formatting | bytes 8388608
Async XLA Ops:
  0.8 1.1 %copy-start = (bf16[128,2176]{1,0:T(8,128)(2,1)S(1)}, bf16[128,2176]{1,0:T(8,128)(2,1)}, u32[]{:S(2)}) copy-start(bf16[128,2176]{1,0:T(8,128)(2,1)} %hid_ref.1) | copy-start | bytes 1671172
  1.8 0.9 %copy-start.1 = (bf16[128,1024]{1,0:T(8,128)(2,1)S(1)}, bf16[128,1024]{1,0:T(8,128)(2,1)}, u32[]{:S(2)}) copy-start(bf16[128,1024]{1,0:T(8,128)(2,1)} %res_ref.1) | copy-start | bytes 786436
  2.8 0.8 %copy-start.2 = (f32[16384]{0:T(1024)S(1)}, f32[16384]{0:T(1024)}, u32[]{:S(2)}) copy-start(f32[16384]{0:T(1024)} %param.8) | copy-start | bytes 196612

commit v3 on v2

--- a/solution.py
+++ b/solution.py
@@ -211,7 +211,7 @@
             multiply(k, h)
             if h == 0:
                 core_copy(k).start()
-        for stage, lag in reversed(stages):
+        for stage, lag in stages:
             if (u - lag) % 2 == 0 and 0 <= (u - lag) // 2 < chunks:
                 stage((u - lag) // 2)
     for k in range(chunks):
@@ -234,7 +234,7 @@
         functools.partial(kernel, nz, ny, width, chunks),
         out_shape=jax.ShapeDtypeStruct((rows, model_width), bf16),
         in_specs=[vmem, vmem, vmem, vmem, pl.BlockSpec(memory_space=pl.ANY)],
-        out_specs=pl.BlockSpec(memory_space=pl.ANY),
+        out_specs=vmem,
         scratch_shapes=[
             pltpu.VMEM((BUFFERS, depth, width), bf16),
             pltpu.VMEM((chunks, ny, nz) + tile, f32),

time: 80.1 us -> 77.6 us (0.969)
  Pallas kernels: 74.2 us -> 71.8 us
    pallas_call x1, Pallas kernels: 74.2 us -> 71.8 us  [shards(): pl.pallas_call(functools.partial(kernel, nz, ny, width, chunks), out_shap...]
where the time goes in v3:
time: 77.6 us; the launch traced here: 77.4 us
  Pallas kernels  71.8 us (93%)
  local copies, waits for them, and re-layouts  5.61 us (7%)
    pallas_call x1, Pallas kernels, shards(): pl.pallas_call(functools.partial(kernel, nz, ny, width, chunks), out_shap...  71.8 us
    unnamed x7, local copies, waits for them, and re-layouts  4.85 us

profile of v3, /device:TPU:0, one launch (start us, length us, event | category | flops | bytes accessed | tf_op | source)
XLA Modules:
  0.0 77.4 jit_solution(15879308361764448808)
XLA Ops:
  0.0 0.8 copy.6.hs_ref
  0.8 0.0 copy-start
  0.8 1.0 %copy-done = bf16[128,2176]{1,0:T(8,128)(2,1)S(1)} copy-done((bf16[128,2176]{1,0:T(8,128)(2,1)S(1)}, bf16[128,2176]{1,0:T(8,128)(2,1)}, u32[]{:S(2)}) %copy-start) | copy-done | bytes 557080
  1.8 0.0 copy-start.1
  1.8 0.9 %copy-done.1 = bf16[128,1024]{1,0:T(8,128)(2,1)S(1)} copy-done((bf16[128,1024]{1,0:T(8,128)(2,1)S(1)}, bf16[128,1024]{1,0:T(8,128)(2,1)}, u32[]{:S(2)}) %copy-start.1) | copy-done | bytes 262168
  2.8 0.0 copy-start.2
  2.8 0.8 %copy-done.2 = f32[16384]{0:T(1024)S(1)} copy-done((f32[16384]{0:T(1024)S(1)}, f32[16384]{0:T(1024)}, u32[]{:S(2)}) %copy-start.2) | copy-done | bytes 65560
  3.6 71.8 %shard_map.55 = bf16[128,16384]{1,0:T(8,128)(2,1)S(1)} custom-call(bf16[128,2176]{1,0:T(8,128)(2,1)S(1)} %copy-done, f32[128,1]{1,0:T(8,128)S(1)} %copy.6.hs_ref, f32[1,16384]{1,0:T(1,128)S(1)} %bitcast.2, bf16[128,1024]{1,0:T(8,128)(2,1)S(1)} %copy-done.1, bf16[2176,16384]{1,0:T(8,128)(2,1)} %w_ref.1), custom_call_target="tpu_custom_call" | custom-call | flops 9126805504 | bytes 71303168 | tf_op jit(solution)/shard_map/pallas_call | solution.py:233
  75.4 2.0 %copy.8 = bf16[128,16384]{1,0:T(8,128)(2,1)} copy(bf16[128,16384]{1,0:T(8,128)(2,1)S(1)} %shard_map.55) | data formatting | bytes 8388608
Async XLA Ops:
  0.8 1.1 %copy-start = (bf16[128,2176]{1,0:T(8,128)(2,1)S(1)}, bf16[128,2176]{1,0:T(8,128)(2,1)}, u32[]{:S(2)}) copy-start(bf16[128,2176]{1,0:T(8,128)(2,1)} %hid_ref.1) | copy-start | bytes 1671172
  1.8 0.9 %copy-start.1 = (bf16[128,1024]{1,0:T(8,128)(2,1)S(1)}, bf16[128,1024]{1,0:T(8,128)(2,1)}, u32[]{:S(2)}) copy-start(bf16[128,1024]{1,0:T(8,128)(2,1)} %res_ref.1) | copy-start | bytes 786436
  2.8 0.8 %copy-start.2 = (f32[16384]{0:T(1024)S(1)}, f32[16384]{0:T(1024)}, u32[]{:S(2)}) copy-start(f32[16384]{0:T(1024)} %param.8) | copy-start | bytes 196612
